TPU v7x, 128 devices: a whole 4x4x4 slice. The times are simulated.
128 devices in a mesh: rx: 4 (over x), ry: 2 (over y_hi), node: 16 (over z, y_lo, core).
Axes of the slice: x: 4, y: 4 (y_hi: 2, y_lo: 2; y = y_hi * 2 + y_lo), z: 4, core: 2. Of those that a mesh axis runs over, the one named last changes fastest.
Arguments:
- activations: bfloat16 [8, 6144, 640], P(('rx', 'ry'), 'node'), may hold values from -6 to 6
- output_grad: bfloat16 [8, 6144, 14336], P(('rx', 'ry'), 'node'), may hold values from -48 to 48
- inner_drift: bfloat16 [8, 640, 14336], P(('rx', 'ry'), 'node'), may hold values from -0.1796875 to 0.1796875
- outer_weights: float32 [640, 14336], P('node', ('rx', 'ry')), may hold values from -0.25 to 0.25
- outer_momentum: float32 [640, 14336], P('node', ('rx', 'ry')), may hold values from -0.12 to 0.12
- next_inputs: bfloat16 [8, 6144, 640], P(('rx', 'ry'), 'node'), may hold values from -6 to 6
Outputs:
- new_weights: float32 [640, 14336], P('node', ('rx', 'ry'))
- new_momentum: float32 [640, 14336], P('node', ('rx', 'ry'))
- next_outputs: bfloat16 [8, 6144, 14336], P(('rx', 'ry'), 'node')
All inputs are finite; a program needn't handle non-finite values.
Results may differ from a plain program's by a relative error of at most 0.02.
Values may be sent and summed in bfloat16 or wider, within the bound.
A program may use at most 128 MiB of HBM per device.

v0:
```python
import jax
import jax.numpy as jnp
from jax import lax
from jax.sharding import PartitionSpec as P

inner_rate = 0.5
outer_rate = 0.7
decay_rate = 0.9


def local(activations, output_grad, inner_drift, outer_weights, outer_momentum, next_inputs):
    node_count = lax.axis_size("node")
    replica_count = lax.axis_size("rx") * lax.axis_size("ry")
    scale = 1.0 / (activations.shape[1] * node_count)
    inputs_now = activations[0]
    grads_now = output_grad[0]
    columns = inputs_now
    product = lax.dot_general(
        columns, grads_now, (((0,), (0,)), ((), ())), preferred_element_type=jnp.float32
    )
    grad_rows = lax.psum_scatter(
        (product * scale).astype(jnp.bfloat16), "node", scatter_dimension=0, tiled=True
    ).astype(jnp.float32)
    local_term = inner_drift[0].astype(jnp.float32) + inner_rate * grad_rows
    summed = lax.psum_scatter(
        local_term.astype(jnp.bfloat16), ("rx", "ry"), scatter_dimension=1, tiled=True
    ).astype(jnp.float32)
    pseudo_grad = summed / replica_count
    new_momentum = decay_rate * outer_momentum + pseudo_grad
    new_weights = outer_weights - outer_rate * (pseudo_grad + decay_rate * new_momentum)
    weights_bf = new_weights.astype(jnp.bfloat16)
    inputs_next = next_inputs[0]
    row_block = lax.all_gather(weights_bf, ("rx", "ry"), axis=1, tiled=True)
    columns = inputs_next
    produced = jnp.dot(
        columns,
        lax.all_gather(row_block, "node", axis=0, tiled=True),
        preferred_element_type=jnp.float32,
    )
    next_outputs = produced.astype(jnp.bfloat16)[None]
    return (new_weights, new_momentum, next_outputs)


def solution(mesh):
    in_specs = (
        P(("rx", "ry"), "node", None),
        P(("rx", "ry"), "node", None),
        P(("rx", "ry"), "node", None),
        P("node", ("rx", "ry")),
        P("node", ("rx", "ry")),
        P(("rx", "ry"), "node", None),
    )
    out_specs = (P("node", ("rx", "ry")), P("node", ("rx", "ry")), P(("rx", "ry"), "node", None))
    return jax.shard_map(local, mesh=mesh, in_specs=in_specs, out_specs=out_specs, check_vma=False)
```

profile of v0, /device:TPU:1, one launch (start us, length us, event | category | flops | bytes accessed | tf_op | source)
XLA Modules:
  0.0 485.0 jit_solution(11664273373380743725)
XLA Ops:
  7.2 0.0 copy-start
  7.2 0.0 reduce-scatter.3.cloned.1.call-start
  7.2 1.0 copy-done
  8.2 16.6 %multiply_convert_fusion = bf16[640,14336]{1,0:T(8,128)(2,1)} fusion(bf16[1,384,14336]{2,1,0:T(8,128)(2,1)} %param.7, bf16[1,384,640]{2,1,0:T(8,128)(2,1)S(1)} %copy-done), kind=kOutput, calls=%fused_computation | convolution fusion | flops 7064780800 | bytes 29851648 | tf_op jit(solution)/shard_map/dot_general | solution.py:18
  24.8 0.0 copy-start.2
  24.8 0.0 copy-start.3
  24.8 0.0 copy-start.4
  24.8 0.0 copy-start.5
  24.8 0.0 reduce-scatter.3.cloned.1.call-update
  24.9 0.0 reduce-scatter.5.cloned.1.call-start
  24.9 199.8 %reduce-scatter.3.cloned.1.call-done = bf16[40,14336]{1,0:T(8,128)(2,1)} async-done(((bf16[640,14336]{1,0:T(8,128)(2,1)}), bf16[40,14336]{1,0:T(8,128)(2,1)}) %reduce-scatter.3.cloned.1.call-update) | async-done | bytes 1146896 | tf_op jit(solution)/shard_map/reduce_scatter | solution.py:21
  224.7 0.0 copy-done.2
  224.7 2.6 fusion.2
  227.3 0.0 reduce-scatter.5.cloned.1.call-update
  227.3 0.0 all-gather.3.cloned.1.call-start
  227.4 68.3 %reduce-scatter.5.cloned.1.call-done = bf16[40,1792]{1,0:T(8,128)(2,1)} async-done(((bf16[40,14336]{1,0:T(8,128)(2,1)}), bf16[40,1792]{1,0:T(8,128)(2,1)}) %reduce-scatter.5.cloned.1.call-update) | async-done | bytes 143376 | tf_op jit(solution)/shard_map/reduce_scatter | solution.py:25
  295.6 0.0 copy-done.3
  295.7 0.0 copy-done.4
  295.7 1.8 fusion.5
  297.5 0.0 all-gather.3.cloned.1.call-update
  297.5 0.0 all-gather.5.cloned.1.call-start
  297.6 47.8 %all-gather.3.cloned.1.call-done = bf16[40,14336]{1,0:T(8,128)(2,1)} async-done(((bf16[40,1792]{1,0:T(8,128)(2,1)}), bf16[40,14336]{1,0:T(8,128)(2,1)}) %all-gather.3.cloned.1.call-update) | async-done | bytes 1146896 | tf_op jit(solution)/shard_map/all_gather | solution.py:33
  345.4 0.0 all-gather.5.cloned.1.call-update
  345.4 101.4 %all-gather.5.cloned.1.call-done = bf16[640,14336]{1,0:T(8,128)(2,1)} async-done(((bf16[40,14336]{1,0:T(8,128)(2,1)}), bf16[640,14336]{1,0:T(8,128)(2,1)}) %all-gather.5.cloned.1.call-update) | async-done | bytes 18350096 | tf_op jit(solution)/shard_map/all_gather | solution.py:37
  446.8 0.0 copy-done.5
  446.8 0.0 copy-start.1
  446.8 17.1 %fusion = bf16[1,384,14336]{1,2,0:T(8,128)(2,1)} fusion(bf16[640,14336]{1,0:T(8,128)(2,1)} %all-gather.5.cloned.1.call-done, bf16[1,384,640]{2,1,0:T(8,128)(2,1)S(1)} %copy-done.5), kind=kOutput, calls=%fused_computation.2 | convolution fusion | flops 7051935744 | bytes 29851648 | tf_op jit(solution)/shard_map/dot_general | solution.py:35
  463.9 14.6 %copy.9 = bf16[1,384,14336]{2,1,0:T(8,128)(2,1)} copy(bf16[1,384,14336]{1,2,0:T(8,128)(2,1)} %fusion) | data formatting | bytes 22020096
  478.5 0.0 copy-done.1
Async XLA Ops:
  7.2 1.0 copy-start
  7.2 217.5 %reduce-scatter.3.cloned.1.call-start = ((), (), s32[]{:S(2)}) async-start(), calls=%async_computation.2 | async-start | bytes 19496960 | tf_op jit(solution)/shard_map/reduce_scatter | solution.py:21
  24.8 199.9 %copy-start.2 = (bf16[1,40,14336]{2,1,0:T(8,128)(2,1)S(1)}, bf16[1,40,14336]{2,1,0:T(8,128)(2,1)}, u32[]{:S(2)}) copy-start(bf16[1,40,14336]{2,1,0:T(8,128)(2,1)} %param.8) | copy-start | bytes 3440644
  24.8 270.8 %copy-start.3 = (f32[40,1792]{1,0:T(8,128)S(1)}, f32[40,1792]{1,0:T(8,128)}, u32[]{:S(2)}) copy-start(f32[40,1792]{1,0:T(8,128)} %param.9) | copy-start | bytes 860164
  24.8 270.8 %copy-start.4 = (f32[40,1792]{1,0:T(8,128)S(1)}, f32[40,1792]{1,0:T(8,128)}, u32[]{:S(2)}) copy-start(f32[40,1792]{1,0:T(8,128)} %param.10) | copy-start | bytes 860164
  24.8 422.0 %copy-start.5 = (bf16[1,384,640]{2,1,0:T(8,128)(2,1)S(1)}, bf16[1,384,640]{2,1,0:T(8,128)(2,1)}, u32[]{:S(2)}) copy-start(bf16[1,384,640]{2,1,0:T(8,128)(2,1)} %param.11) | copy-start | bytes 1474564
  24.9 270.8 %reduce-scatter.5.cloned.1.call-start = ((), (), s32[]{:S(2)}) async-start(), calls=%async_computation.3 | async-start | bytes 1290240 | tf_op jit(solution)/shard_map/reduce_scatter | solution.py:25
  227.3 118.1 %all-gather.3.cloned.1.call-start = ((), (), s32[]{:S(2)}) async-start(), calls=%async_computation.4 | async-start | bytes 1290240 | tf_op jit(solution)/shard_map/all_gather | solution.py:33
  297.5 149.3 %all-gather.5.cloned.1.call-start = ((), (), s32[]{:S(2)}) async-start(), calls=%async_computation.5 | async-start | bytes 19496960 | tf_op jit(solution)/shard_map/all_gather | solution.py:37
  446.8 31.7 %copy-start.1 = (bf16[1,384,640]{2,1,0:T(8,128)(2,1)S(1)}, bf16[1,384,640]{2,1,0:T(8,128)(2,1)}, u32[]{:S(2)}) copy-start(bf16[1,384,640]{2,1,0:T(8,128)(2,1)} %param.6) | copy-start | bytes 1474564
Sparse Core Ops, SparseCore 0:
  25.0 199.6 reduce-scatter.2
  228.9 66.7 reduce-scatter.4
  298.6 46.7 all-gather.2
  347.0 99.8 all-gather.4
where the time goes:
time: 486 us; the launch traced here: 485 us
  waiting for transfers between devices  417 us (86%)
  matrix products  33.7 us (7%)
  local copies, waits for them, and re-layouts  15.6 us (3%)
  between operations  13.8 us (3%)
    reduce_scatter x1, waiting for transfers between devices, local(): lax.psum_scatter((product * scale).astype(jnp.bfloat16), 'node', scatter_...  200 us
    all_gather x1, waiting for transfers between devices, local(): lax.all_gather(row_block, 'node', axis=0, tiled=True)  101 us
    reduce_scatter x1, waiting for transfers between devices, local(): lax.psum_scatter(local_term.astype(jnp.bfloat16), ('rx', 'ry'), scatter_d...  68.3 us
    all_gather x1, waiting for transfers between devices, local(): row_block = lax.all_gather(weights_bf, ('rx', 'ry'), axis=1, tiled=True)  47.8 us
    dot_general x1, matrix products, local(): jnp.dot(columns, lax.all_gather(row_block, 'node', axis=0, tiled=True), p...  17.1 us
    dot_general x1, matrix products, local(): lax.dot_general(columns, grads_now, (((0,), (0,)), ((), ())), preferred_e...  16.6 us
    unnamed x13, local copies, waits for them, and re-layouts  15.6 us
  transfers between devices with their start and end apart: 4, of which 4 were waited for; matrix products, arithmetic and copies ran while one was open for 0% of the time, Pallas kernels for 0%

commit v1 on v0

v1 whole, which is shorter than its diff:
```python
import functools

import jax
import jax.numpy as jnp
from jax import lax
from jax.experimental import pallas as pl
from jax.experimental.pallas import tpu as pltpu
from jax.sharding import PartitionSpec as P

inner_rate = 0.5
outer_rate = 0.7
decay_rate = 0.9

MESH = pl.DeviceIdType.MESH
BF = jnp.bfloat16
F32 = jnp.float32

CHUNKS = (
    (0, 384, (("xyz", 0, 128, 0, 80), ("yzx", 128, 128, 0, 80), ("zxy", 256, 128, 0, 80))),
    (
        384,
        512,
        (
            ("xyz", 384, 128, 0, 80),
            ("yzx", 512, 128, 0, 80),
            ("zxy", 640, 128, 0, 80),
            ("xyz", 768, 128, 0, 32),
            ("yzx", 768, 128, 32, 32),
            ("zxy", 768, 128, 64, 16),
        ),
    ),
)
PARTS = tuple(part for _, _, parts in CHUNKS for part in parts)


def place():
    n = lax.axis_index("node")
    return {
        "x": lax.axis_index("rx"),
        "y": lax.axis_index("ry") * 2 + (n // 2) % 2,
        "z": n // 4,
        "c": n % 2,
    }


def device(at):
    return (at["x"], at["y"] // 2, (at["z"] * 2 + at["y"] % 2) * 2 + at["c"])


def step(at, axis, by):
    return {**at, axis: (at[axis] + by) % 4}


def index(axes, sel):
    def one(axis):
        s = sel.get(axis)
        if s is None:
            return slice(None)
        return pl.ds(2 * s[1], 2) if isinstance(s, tuple) else s

    y = sel.get("y")
    out = [one("x")] if "x" in axes else []
    if "y" in axes:
        out.append(slice(None) if y is None else y[1] if isinstance(y, tuple) else y // 2)
    if "z" in axes:
        out.append(one("z"))
    if "y" in axes:
        out.append(slice(None) if y is None or isinstance(y, tuple) else y % 2)
    return tuple(out)


def dims(axes, tail):
    shape = (4,) if "x" in axes else ()
    shape += (2,) if "y" in axes else ()
    shape += (4,) if "z" in axes else ()
    shape += (2,) if "y" in axes else ()
    return shape + tail


def ordered(axes):
    return "".join(axis for axis in "xyz" if axis in axes)


def sync_kernel(*refs):
    np_ = len(PARTS)
    act, grad, drift, w_in, m_in = refs[:5]
    nw_out, nm_out = refs[5:7]
    w_out = refs[7 : 7 + np_]
    rest = list(refs[7 + np_ :])
    a_own, a_sib, at_buf, dr_own, dr_sib, dr32, ow, om, nw, nm = rest[:10]
    del rest[:10]
    g_buf = [rest.pop(0) for _ in CHUNKS]
    p_buf = [rest.pop(0) for _ in PARTS]
    stage = [rest.pop(0) for _ in PARTS]
    ring = [[[rest.pop(0) for _ in range(3)] for _ in range(3)] for _ in PARTS]
    send, recv, local = rest

    at = place()
    h = at["c"]
    sib = {**at, "c": 1 - h}
    rows_own = pl.multiple_of(h * 40, 8)
    rows_sib = pl.multiple_of((1 - h) * 40, 8)
    count = {"r": 0, "l": 0}
    pending = []

    def remote(src, dst, to):
        k = count["r"]
        count["r"] += 1
        copy = pltpu.make_async_remote_copy(
            src, dst, send.at[k], recv.at[k], device_id=device(to), device_id_type=MESH
        )
        copy.start()
        pending.append(copy)
        return copy

    def near(src, dst):
        k = count["l"]
        count["l"] += 1
        copy = pltpu.make_async_copy(src, dst, local.at[k])
        copy.start()
        return copy

    load_act = near(act.at[0], a_own)
    load_g = []
    for k, (c0, wc, _) in enumerate(CHUNKS):
        load_g.append(
            [
                near(
                    grad.at[0, :, pl.ds(pl.multiple_of(q * 1792 + h * 896 + c0, 128), wc)],
                    g_buf[k].at[q, pl.ds(0, 384)],
                )
                for q in range(8)
            ]
        )
    load_dr = [
        near(drift.at[0, :, pl.ds(pl.multiple_of(q * 1792 + h * 896, 128), 896)], dr_own.at[q])
        for q in range(8)
    ]
    col_own = pl.ds(pl.multiple_of(h * 896, 128), 896)
    col_sib = pl.ds(pl.multiple_of((1 - h) * 896, 128), 896)
    load_ow = near(w_in.at[:, col_own], ow.at[pl.ds(rows_own, 40)])
    load_om = near(m_in.at[:, col_own], om.at[pl.ds(rows_own, 40)])

    barrier = pltpu.get_barrier_semaphore()
    others = [sib] + [step(at, axis, by) for axis in "xyz" for by in (1, 2, 3)]
    for to in others:
        pl.semaphore_signal(barrier, 1, device_id=device(to), device_id_type=MESH)
    pl.semaphore_wait(barrier, len(others))

    send_act = remote(act.at[0], a_sib, sib)
    send_g = []
    for k, (c0, wc, _) in enumerate(CHUNKS):
        send_g.append(
            [
                remote(
                    grad.at[0, :, pl.ds(pl.multiple_of(q * 1792 + (1 - h) * 896 + c0, 128), wc)],
                    g_buf[k].at[q, pl.ds(384, 384)],
                    sib,
                )
                for q in range(8)
            ]
        )
        if k == 0:
            send_dr = [
                remote(
                    drift.at[0, :, pl.ds(pl.multiple_of(q * 1792 + (1 - h) * 896, 128), 896)],
                    dr_sib.at[q],
                    sib,
                )
                for q in range(8)
            ]
    send_ow = remote(w_in.at[:, col_sib], ow.at[pl.ds(rows_own, 40)], sib)
    send_om = remote(m_in.at[:, col_sib], om.at[pl.ds(rows_own, 40)], sib)

    load_act.wait()
    for i in range(5):
        at_buf[pl.ds(i * 128, 128), pl.ds(0, 384)] = a_own[:, pl.ds(i * 128, 128)].T
    send_act.wait_recv()
    for i in range(5):
        at_buf[pl.ds(i * 128, 128), pl.ds(384, 384)] = a_sib[:, pl.ds(i * 128, 128)].T

    scale = inner_rate / (384 * 16)

    def product(k):
        c0, wc, parts = CHUNKS[k]
        for copy in load_g[k]:
            copy.wait()
        for copy in send_g[k]:
            copy.wait_recv()
        if k == 0:
            for copy in load_dr:
                copy.wait()
            for copy in send_dr:
                copy.wait_recv()
            load_ow.wait()
            load_om.wait()
            send_ow.wait_recv()
            send_om.wait_recv()

            @pl.loop(0, 8)
            def _(q):
                dr32[q, pl.ds(rows_own, 40)] = dr_own[q].astype(F32)
                dr32[q, pl.ds(rows_sib, 40)] = dr_sib[q].astype(F32)

        @pl.loop(0, 8)
        def _(q):
            total = jnp.dot(at_buf[...], g_buf[k][q], preferred_element_type=F32)
            value = (total * scale).astype(BF)
            for part in parts:
                order, pc, w, r0, rows = part
                ref = p_buf[PARTS.index(part)]
                block = value[:, pc - c0 : pc - c0 + w].reshape(4, 2, 80, w)
                ref[q // 2, q % 2] = block[:, :, r0 : r0 + rows]
                mine = (q // 2, q % 2, at["z"], at["y"] % 2)
                ref[mine] = (
                    ref[mine].astype(F32) + dr32[q, pl.ds(r0, rows), pl.ds(pc, w)]
                ).astype(BF)

    def tiles(axes, half_axis, half, body):
        n = 4 ** len(axes) // (1 if half_axis is None else 2)

        @pl.loop(0, n)
        def _(i):
            sel = {}
            for axis in axes:
                if axis == half_axis:
                    sel[axis] = 2 * half + i % 2
                    i = i // 2
                else:
                    sel[axis] = i % 4
                    i = i // 4
            body(sel)

    def pipeline(s):
        order, pc, w, r0, rows = PARTS[s]
        p, wo, st = p_buf[s], w_out[s], stage[s]
        fixed = {}
        for phase in range(2):
            axis = order[phase]
            left_axes = ordered(order[phase + 1 :])
            split = order[-1]
            via, from_left, from_right = ring[s][phase]
            m = at[axis]
            right, left = step(at, axis, 1), step(at, axis, 3)

            def block(dest, half):
                return p.at[index("xyz", {**fixed, axis: dest % 4, split: ("half", half)})]

            def part_of(ref, half):
                return ref.at[index(left_axes, {split: ("half", half)})]

            v0 = remote(block(m + 2, 0), part_of(via, 0), right)
            v1 = remote(block(m + 2, 1), part_of(via, 1), left)
            e0 = remote(block(m + 1, 1), part_of(from_left, 1), right)
            e1 = remote(block(m + 3, 0), part_of(from_right, 0), left)
            yield
            v0.wait_recv()
            v1.wait_recv()
            for half, dest in ((0, m + 1), (1, m + 3)):

                def add(sel):
                    i = index("xyz", {**fixed, **sel, axis: dest % 4})
                    p[i] = (p[i].astype(F32) + via[index(left_axes, sel)].astype(F32)).astype(BF)

                tiles(left_axes, split, half, add)
            l0 = remote(block(m + 1, 0), part_of(from_left, 0), right)
            l1 = remote(block(m + 3, 1), part_of(from_right, 1), left)
            yield
            for copy in (e0, e1, l0, l1):
                copy.wait_recv()

            def total(sel):
                i = index("xyz", {**fixed, **sel, axis: m})
                j = index(left_axes, sel)
                p[i] = (
                    p[i].astype(F32) + (from_left[j].astype(F32) + from_right[j].astype(F32))
                ).astype(BF)

            tiles(left_axes, None, 0, total)
            fixed[axis] = m
        axis = order[2]
        bufs = ring[s][2]
        got = [
            remote(
                p.at[index("xyz", {**fixed, axis: (at[axis] + by) % 4})],
                bufs[by - 1],
                step(at, axis, by),
            )
            for by in (1, 2, 3)
        ]
        yield
        for copy in got:
            copy.wait_recv()
        me = {"x": at["x"], "y": at["y"], "z": at["z"]}
        mine = index("xyz", me)
        summed = p[mine].astype(F32)
        for ref in bufs:
            summed = summed + ref[...].astype(F32)
        pseudo = summed * 0.125
        area = (pl.ds(r0, rows), pl.ds(pc, w))
        momentum = decay_rate * om[area] + pseudo
        weights = ow[area] - outer_rate * (pseudo + decay_rate * momentum)
        nm[area] = momentum
        nw[area] = weights
        st[...] = weights.astype(BF)

        def tile(sel):
            return wo.at[(h,) + index("xyz", sel)]

        keep = near(st, tile(me))
        got = [remote(st, tile(me), step(at, axis, by)) for by in (1, 2, 3)]
        yield
        keep.wait()
        for copy in got:
            copy.wait_recv()
        across = []
        for phase in (1, 0):
            axis = order[phase]
            split = order[-1]
            del fixed[axis]
            m = at[axis]
            right, left = step(at, axis, 1), step(at, axis, 3)

            def part(pos, half=None):
                sel = {**fixed, axis: pos % 4}
                if half is not None:
                    sel[split] = ("half", half)
                return tile(sel)

            r = remote(part(m), part(m), right)
            l = remote(part(m), part(m), left)
            if phase == 0:
                across.append(remote(part(m), part(m), sib))
            yield
            r.wait_recv()
            fr = remote(part(m + 3, 0), part(m + 3, 0), right)
            l.wait_recv()
            fl = remote(part(m + 1, 1), part(m + 1, 1), left)
            if phase == 0:
                across.append(remote(part(m + 3), part(m + 3), sib))
                across.append(remote(part(m + 1), part(m + 1), sib))
            yield
            fr.wait_recv()
            fl.wait_recv()
        across.append(remote(part(m + 2), part(m + 2), sib))
        yield
        for copy in across:
            copy.wait_recv()

    runs = []
    first = 0
    for _, _, parts in CHUNKS:
        runs.append([pipeline(first + i) for i in range(len(parts))])
        first += len(parts)

    def go(k, n=1):
        for _ in range(n):
            for run in runs[k]:
                next(run, None)

    schedule(product, go)

    back = [
        remote(nw.at[pl.ds(rows_sib, 40)], nw_out.at[:, col_own], sib),
        remote(nm.at[pl.ds(rows_sib, 40)], nm_out.at[:, col_own], sib),
    ]
    keep = [
        near(nw.at[pl.ds(rows_own, 40)], nw_out.at[:, col_own]),
        near(nm.at[pl.ds(rows_own, 40)], nm_out.at[:, col_own]),
    ]
    for k in range(len(CHUNKS)):
        go(k)
    for copy in keep:
        copy.wait()
    for copy in back:
        copy.wait_recv()
    for copy in pending:
        copy.wait_send()


def schedule(product, go):
    product(0)
    go(0)
    product(1)
    go(0)
    go(1)
    go(0)
    go(0)
    go(0)
    go(1)
    go(0)
    go(0)
    go(1)
    go(0)
    go(1)
    go(0)
    go(1)
    go(1)
    go(0)
    go(1)
    go(1)
    go(0)
    go(1)
    go(1)
    go(1)


def out_kernel(*refs):
    np_ = len(PARTS)
    x_ref = refs[0]
    w_refs = refs[1 : 1 + np_]
    o_ref = refs[1 + np_]
    strips = {}
    for part, ref in zip(PARTS, w_refs):
        strips.setdefault((part[1], part[2]), []).append((part[3], part[4], ref))
    columns = []
    for key in sorted(strips):
        rows = [ref[...].reshape(8, n, key[1]) for _, n, ref in sorted(strips[key], key=lambda t: t[0])]
        block = rows[0] if len(rows) == 1 else jnp.concatenate(rows, axis=1)
        columns.append(block.reshape(640, key[1]))
    weights = jnp.concatenate(columns, axis=1)
    o_ref[...] = jnp.dot(x_ref[...], weights, preferred_element_type=F32).astype(BF)[None]


def local(activations, output_grad, inner_drift, outer_weights, outer_momentum, next_inputs):
    any_ = pl.BlockSpec(memory_space=pl.ANY)
    w_shapes = [
        jax.ShapeDtypeStruct((2,) + dims("xyz", (rows, w)), BF) for _, _, w, _, rows in PARTS
    ]
    scratch = [
        pltpu.VMEM((384, 640), BF),
        pltpu.VMEM((384, 640), BF),
        pltpu.VMEM((640, 768), BF),
        pltpu.VMEM((8, 40, 896), BF),
        pltpu.VMEM((8, 40, 896), BF),
        pltpu.VMEM((8, 80, 896), F32),
    ]
    scratch += [pltpu.VMEM((80, 896), F32)] * 4
    scratch += [pltpu.VMEM((8, 768, wc), BF) for _, wc, _ in CHUNKS]
    scratch += [pltpu.VMEM(dims("xyz", (rows, w)), BF) for _, _, w, _, rows in PARTS]
    scratch += [pltpu.VMEM((rows, w), BF) for _, _, w, _, rows in PARTS]
    for order, _, w, _, rows in PARTS:
        for phase in range(3):
            scratch += [pltpu.VMEM(dims(ordered(order[phase + 1 :]), (rows, w)), BF)] * 3
    n_remote = 1 + 8 * len(CHUNKS) + 8 + 2 + 2 + len(PARTS) * (15 + 3 + 8 + 4)
    n_local = 1 + 8 * len(CHUNKS) + 8 + 2 + 2 + len(PARTS)
    scratch += [
        pltpu.SemaphoreType.DMA((n_remote,)),
        pltpu.SemaphoreType.DMA((n_remote,)),
        pltpu.SemaphoreType.DMA((n_local,)),
    ]
    state = jax.ShapeDtypeStruct((40, 1792), F32)
    results = pl.pallas_call(
        sync_kernel,
        out_shape=[state, state] + w_shapes,
        in_specs=[any_] * 5,
        out_specs=[any_] * (2 + len(PARTS)),
        scratch_shapes=scratch,
        compiler_params=pltpu.CompilerParams(
            collective_id=0, has_side_effects=True, vmem_limit_bytes=60 * 2**20
        ),
        name="sync",
    )(activations, output_grad, inner_drift, outer_weights, outer_momentum)
    new_weights, new_momentum, w_all = results[0], results[1], results[2:]

    def w_spec(part):
        _, _, w, _, rows = part
        return pl.BlockSpec(
            (None, None, None, 4, 2, rows, w), lambda q, h: (h, q // 2, q % 2, 0, 0, 0, 0)
        )

    next_outputs = pl.pallas_call(
        out_kernel,
        out_shape=jax.ShapeDtypeStruct((1, 384, 14336), BF),
        grid=(8, 2),
        in_specs=[pl.BlockSpec((384, 640), lambda q, h: (0, 0))] + [w_spec(p) for p in PARTS],
        out_specs=pl.BlockSpec((1, 384, 896), lambda q, h: (0, 0, q * 2 + h)),
        compiler_params=pltpu.CompilerParams(vmem_limit_bytes=32 * 2**20),
        name="outputs",
    )(next_inputs[0], *w_all)
    return new_weights, new_momentum, next_outputs


def solution(mesh):
    in_specs = (
        P(("rx", "ry"), "node", None),
        P(("rx", "ry"), "node", None),
        P(("rx", "ry"), "node", None),
        P("node", ("rx", "ry")),
        P("node", ("rx", "ry")),
        P(("rx", "ry"), "node", None),
    )
    out_specs = (P("node", ("rx", "ry")), P("node", ("rx", "ry")), P(("rx", "ry"), "node", None))
    return jax.shard_map(local, mesh=mesh, in_specs=in_specs, out_specs=out_specs, check_vma=False)
```

time: 486 us -> 148 us (0.30)
  waiting for transfers between devices: 417 us -> 0 us
  Pallas kernels: 0 us -> 131 us
  matrix products: 33.7 us -> 0 us
  between operations: 13.8 us -> 0.68 us
    reduce_scatter x2 -> x0, waiting for transfers between devices: 268 us -> none  [the longest x1 200 us: local(): lax.psum_scatter((product * scale).astype(jnp.bfloat16), 'node', scatter_...]
    all_gather x2 -> x0, waiting for transfers between devices: 149 us -> none  [the longest x1 101 us: local(): lax.all_gather(row_block, 'node', axis=0, tiled=True)]
    pallas_call x0 -> x2, Pallas kernels: none -> 131 us  [the longest x1 118 us: local(): pl.pallas_call(sync_kernel, out_shape=[state, state] + w_shapes, in_specs...]
    dot_general x2 -> x0, matrix products: 33.7 us -> none  [the longest x1 17.1 us: local(): jnp.dot(columns, lax.all_gather(row_block, 'node', axis=0, tiled=True), p...]
    unnamed x13 -> x26, local copies, waits for them, and re-layouts: 15.6 us -> 15.4 us
  transfers between devices with their start and end apart: 4 -> 0, of which waited for: 4 -> 0; matrix products, arithmetic and copies ran while one was open for 0% -> 0% of each run, Pallas kernels for 0% -> 0%
where the time goes in v1:
time: 148 us; the launch traced here: 147 us
  Pallas kernels  131 us (89%)
  local copies, waits for them, and re-layouts  15.4 us (10%)
    pallas_call x1, Pallas kernels, local(): pl.pallas_call(sync_kernel, out_shape=[state, state] + w_shapes, in_specs...  118 us
    unnamed x26, local copies, waits for them, and re-layouts  15.4 us
    pallas_call x1, Pallas kernels, local(): pl.pallas_call(out_kernel, out_shape=jax.ShapeDtypeStruct((1, 384, 14336)...  13.5 us

profile of v1, /device:TPU:1, one launch (start us, length us, event | category | flops | bytes accessed | tf_op | source)
XLA Modules:
  0.0 147.3 jit_solution(13119296440817336097)
XLA Ops:
  0.6 0.0 copy-start.9
  0.6 117.8 %sync.1 = (f32[40,1792]{1,0:T(8,128)}, f32[40,1792]{1,0:T(8,128)}, bf16[2,4,2,4,2,80,128]{6,5,4,3,2,1,0:T(8,128)(2,1)}, bf16[2,4,2,4,2,80,128]{6,5,4,3,2,1,0:T(8...) custom-call(bf16[1,384,640]{2,1,0:T(8,128)(2,1)} %refs_0_.1, ...), custom_call_target="tpu_custom_call" | custom-call | tf_op jit(solution)/shard_map/sync/pallas_call | solution.py:453
  118.4 0.0 copy-done.9
  118.4 0.0 copy-start
  118.4 1.7 %copy-done = bf16[2,4,2,4,2,80,128]{6,5,4,3,2,1,0:T(8,128)(2,1)S(1)} copy-done((bf16[2,4,2,4,2,80,128]{6,5,4,3,2,1,0:T(8,128)(2,1)S(1)}, bf16[2,4,2,4,2,80,128]{6,5,4,3,2,1,0:T(8,128)(2,1)}, u32[]{:S(2)}) %copy-start) | copy-done | bytes 2621464
  120.2 0.0 copy-start.1
  120.2 1.7 %copy-done.1 = bf16[2,4,2,4,2,80,128]{6,5,4,3,2,1,0:T(8,128)(2,1)S(1)} copy-done((bf16[2,4,2,4,2,80,128]{6,5,4,3,2,1,0:T(8,128)(2,1)S(1)}, bf16[2,4,2,4,2,80,128]{6,5,4,3,2,1,0:T(8,128)(2,1)}, u32[]{:S(2)}) %copy-start.1) | copy-done | bytes 2621464
  121.9 0.0 copy-start.2
  121.9 1.7 %copy-done.2 = bf16[2,4,2,4,2,80,128]{6,5,4,3,2,1,0:T(8,128)(2,1)S(1)} copy-done((bf16[2,4,2,4,2,80,128]{6,5,4,3,2,1,0:T(8,128)(2,1)S(1)}, bf16[2,4,2,4,2,80,128]{6,5,4,3,2,1,0:T(8,128)(2,1)}, u32[]{:S(2)}) %copy-start.2) | copy-done | bytes 2621464
  123.7 0.0 copy-start.3
  123.7 1.7 %copy-done.3 = bf16[2,4,2,4,2,80,128]{6,5,4,3,2,1,0:T(8,128)(2,1)S(1)} copy-done((bf16[2,4,2,4,2,80,128]{6,5,4,3,2,1,0:T(8,128)(2,1)S(1)}, bf16[2,4,2,4,2,80,128]{6,5,4,3,2,1,0:T(8,128)(2,1)}, u32[]{:S(2)}) %copy-start.3) | copy-done | bytes 2621464
  125.4 0.0 copy-start.4
  125.4 1.7 %copy-done.4 = bf16[2,4,2,4,2,80,128]{6,5,4,3,2,1,0:T(8,128)(2,1)S(1)} copy-done((bf16[2,4,2,4,2,80,128]{6,5,4,3,2,1,0:T(8,128)(2,1)S(1)}, bf16[2,4,2,4,2,80,128]{6,5,4,3,2,1,0:T(8,128)(2,1)}, u32[]{:S(2)}) %copy-start.4) | copy-done | bytes 2621464
  127.1 0.0 copy-start.5
  127.1 1.7 %copy-done.5 = bf16[2,4,2,4,2,80,128]{6,5,4,3,2,1,0:T(8,128)(2,1)S(1)} copy-done((bf16[2,4,2,4,2,80,128]{6,5,4,3,2,1,0:T(8,128)(2,1)S(1)}, bf16[2,4,2,4,2,80,128]{6,5,4,3,2,1,0:T(8,128)(2,1)}, u32[]{:S(2)}) %copy-start.5) | copy-done | bytes 2621464
  128.9 0.0 copy-start.6
  128.9 1.2 copy-done.6
  130.1 0.0 copy-start.7
  130.1 1.2 copy-done.7
  131.3 0.0 copy-start.8
  131.3 1.0 copy-done.8
  132.4 0.0 copy-start.11
  132.4 0.0 copy-start.10
  132.4 13.5 %outputs.1 = bf16[1,384,14336]{2,1,0:T(8,128)(2,1)} custom-call(bf16[384,640]{1,0:T(8,128)(2,1)S(1)} %bitcast.1, bf16[2,4,2,4,2,80,128]{6,5,4,3,2,1,0:T(8,128)(2,1)S(1)} %copy-done, bf16[2,4,2,4,2,80,128]{6,5,4,3,2,1,0:T(8,128)(2,1)S(1)} %copy-done.1, bf16[2,4,2,4,2,80,128]{6,5,4,3,2,1,0:T(8,128)(2,1)S(1)} %copy-done.2, ...), custom_call_target="tpu_custom_call" | custom-call | tf_op jit(solution)/shard_map/outputs/pallas_call | solution.py:472
  145.9 0.0 copy-done.11
  145.9 0.7 copy.11
  146.6 0.0 copy-done.10
  146.6 0.7 copy.12
Async XLA Ops:
  0.6 117.8 %copy-start.9 = (bf16[1,384,640]{2,1,0:T(8,128)(2,1)S(1)}, bf16[1,384,640]{2,1,0:T(8,128)(2,1)}, u32[]{:S(2)}) copy-start(bf16[1,384,640]{2,1,0:T(8,128)(2,1)} %param.11) | copy-start | bytes 1474564
  118.4 1.7 %copy-start = (bf16[2,4,2,4,2,80,128]{6,5,4,3,2,1,0:T(8,128)(2,1)S(1)}, bf16[2,4,2,4,2,80,128]{6,5,4,3,2,1,0:T(8,128)(2,1)}, u32[]{:S(2)}) copy-start(bf16[2,4,2,4,2,80,128]{6,5,4,3,2,1,0:T(8,128)(2,1)} %get-tuple-element.16.refs_1_) | copy-start | bytes 7864324
  120.2 1.7 %copy-start.1 = (bf16[2,4,2,4,2,80,128]{6,5,4,3,2,1,0:T(8,128)(2,1)S(1)}, bf16[2,4,2,4,2,80,128]{6,5,4,3,2,1,0:T(8,128)(2,1)}, u32[]{:S(2)}) copy-start(bf16[2,4,2,4,2,80,128]{6,5,4,3,2,1,0:T(8,128)(2,1)} %get-tuple-element.17.refs_2_) | copy-start | bytes 7864324
  121.9 1.7 %copy-start.2 = (bf16[2,4,2,4,2,80,128]{6,5,4,3,2,1,0:T(8,128)(2,1)S(1)}, bf16[2,4,2,4,2,80,128]{6,5,4,3,2,1,0:T(8,128)(2,1)}, u32[]{:S(2)}) copy-start(bf16[2,4,2,4,2,80,128]{6,5,4,3,2,1,0:T(8,128)(2,1)} %get-tuple-element.18.refs_3_) | copy-start | bytes 7864324
  123.7 1.7 %copy-start.3 = (bf16[2,4,2,4,2,80,128]{6,5,4,3,2,1,0:T(8,128)(2,1)S(1)}, bf16[2,4,2,4,2,80,128]{6,5,4,3,2,1,0:T(8,128)(2,1)}, u32[]{:S(2)}) copy-start(bf16[2,4,2,4,2,80,128]{6,5,4,3,2,1,0:T(8,128)(2,1)} %get-tuple-element.19.refs_4_) | copy-start | bytes 7864324
  125.4 1.7 %copy-start.4 = (bf16[2,4,2,4,2,80,128]{6,5,4,3,2,1,0:T(8,128)(2,1)S(1)}, bf16[2,4,2,4,2,80,128]{6,5,4,3,2,1,0:T(8,128)(2,1)}, u32[]{:S(2)}) copy-start(bf16[2,4,2,4,2,80,128]{6,5,4,3,2,1,0:T(8,128)(2,1)} %get-tuple-element.20.refs_5_) | copy-start | bytes 7864324
  127.1 1.7 %copy-start.5 = (bf16[2,4,2,4,2,80,128]{6,5,4,3,2,1,0:T(8,128)(2,1)S(1)}, bf16[2,4,2,4,2,80,128]{6,5,4,3,2,1,0:T(8,128)(2,1)}, u32[]{:S(2)}) copy-start(bf16[2,4,2,4,2,80,128]{6,5,4,3,2,1,0:T(8,128)(2,1)} %get-tuple-element.21.refs_6_) | copy-start | bytes 7864324
  128.9 1.2 copy-start.6
  130.1 1.2 copy-start.7
  131.3 1.0 copy-start.8
  132.4 13.5 %copy-start.11 = (f32[40,1792]{1,0:T(8,128)S(1)}, f32[40,1792]{1,0:T(8,128)}, u32[]{:S(2)}) copy-start(f32[40,1792]{1,0:T(8,128)} %get-tuple-element.28) | copy-start | bytes 860164
  132.4 14.2 %copy-start.10 = (f32[40,1792]{1,0:T(8,128)S(1)}, f32[40,1792]{1,0:T(8,128)}, u32[]{:S(2)}) copy-start(f32[40,1792]{1,0:T(8,128)} %get-tuple-element.29) | copy-start | bytes 860164

commit v2 on v1

v2 whole, which is shorter than its diff:
```python
import functools

import jax
import jax.numpy as jnp
from jax import lax
from jax.experimental import pallas as pl
from jax.experimental.pallas import tpu as pltpu
from jax.sharding import PartitionSpec as P

inner_rate = 0.5
outer_rate = 0.7
decay_rate = 0.9

MESH = pl.DeviceIdType.MESH
BF = jnp.bfloat16
F32 = jnp.float32

CHUNKS = (
    (0, 384, (("xyz", 0, 128, 0, 80), ("yzx", 128, 128, 0, 80), ("zxy", 256, 128, 0, 80))),
    (768, 128, (("xyz", 768, 128, 0, 32), ("yzx", 768, 128, 32, 32), ("zxy", 768, 128, 64, 16))),
    (384, 384, (("xyz", 384, 128, 0, 80), ("yzx", 512, 128, 0, 80), ("zxy", 640, 128, 0, 80))),
)
PARTS = tuple(part for _, _, parts in CHUNKS for part in parts)
PLACES = {0: (0, 384), 1: (384, 128)}
ORDER = (
    "p0", "s0", "p1", "s1", "s0", "s0", "s1", "s1", "p2", "s0", "s1", "s0", "s2", "s1", "s0",
    "s2", "s0", "s1", "s2", "s1", "s0", "s2", "s0", "s1", "s2", "s0", "s1", "s2", "s0", "s2",
    "b0", "s0", "s0", "s2", "s1", "s0", "s2", "s1", "s1", "s2", "s2", "s1", "s0", "s1", "l0",
    "s2", "m004", "s1", "m102", "s2", "m046", "m126", "s2", "m168", "m068", "s2",
)
PRODUCTS = tuple(int(word[1]) for word in ORDER if word[0] == "p")


def place():
    n = lax.axis_index("node")
    return {
        "x": lax.axis_index("rx"),
        "y": lax.axis_index("ry") * 2 + (n // 2) % 2,
        "z": n // 4,
        "c": n % 2,
    }


def device(at):
    return (at["x"], at["y"] // 2, (at["z"] * 2 + at["y"] % 2) * 2 + at["c"])


def step(at, axis, by):
    return {**at, axis: (at[axis] + by) % 4}


def index(axes, sel):
    def one(axis):
        s = sel.get(axis)
        if s is None:
            return slice(None)
        return pl.ds(2 * s[1], 2) if isinstance(s, tuple) else s

    y = sel.get("y")
    out = [one("x")] if "x" in axes else []
    if "y" in axes:
        out.append(slice(None) if y is None else y[1] if isinstance(y, tuple) else y // 2)
    if "z" in axes:
        out.append(one("z"))
    if "y" in axes:
        out.append(slice(None) if y is None or isinstance(y, tuple) else y % 2)
    return tuple(out)


def dims(axes, tail):
    shape = (4,) if "x" in axes else ()
    shape += (2,) if "y" in axes else ()
    shape += (4,) if "z" in axes else ()
    shape += (2,) if "y" in axes else ()
    return shape + tail


def ordered(axes):
    return "".join(axis for axis in "xyz" if axis in axes)


def weights_of(parts, refs, q):
    strips = {}
    for part, ref in zip(parts, refs):
        strips.setdefault((part[1], part[2]), []).append((part[3], part[4], ref))
    lanes = []
    for half in range(2):
        for key in sorted(strips):
            rows = [
                ref[half, q // 2, q % 2].reshape(8, n, key[1])
                for _, n, ref in sorted(strips[key], key=lambda t: t[0])
            ]
            block = rows[0] if len(rows) == 1 else jnp.concatenate(rows, axis=1)
            lanes.append(block.reshape(640, key[1]))
    return jnp.concatenate(lanes, axis=1)


def sync_kernel(*refs):
    act, grad, drift, w_in, m_in, x_in = refs[:6]
    nw_out, nm_out, x_buf, o_out = refs[6:10]
    rest = list(refs[10:])
    w_far = [rest.pop(0) for _ in CHUNKS[0][2]]
    w_last = [rest.pop(0) for _ in CHUNKS[2][2]]
    a_own, a_sib, at_buf, dr32, ow, om, nw, nm = rest[:8]
    del rest[:8]
    w_mid = [rest.pop(0) for _ in CHUNKS[1][2]]
    w_out = w_far + w_mid + w_last
    w_load = [rest.pop(0) for _ in CHUNKS[0][2]]
    dr_own = [rest.pop(0) for _ in CHUNKS]
    dr_sib = [rest.pop(0) for _ in CHUNKS]
    g_buf = [rest.pop(0) for _ in CHUNKS]
    p_buf = [rest.pop(0) for _ in PARTS]
    stage = [rest.pop(0) for _ in PARTS]
    ring = [[[rest.pop(0) for _ in range(3)] for _ in range(3)] for _ in PARTS]
    send, recv, local, load, w_sem = rest

    at = place()
    h = at["c"]
    sib = {**at, "c": 1 - h}
    rows_own = pl.multiple_of(h * 40, 8)
    rows_sib = pl.multiple_of((1 - h) * 40, 8)
    count = {"r": 0, "l": 0}
    pending = []

    def remote(src, dst, to, start=True):
        k = count["r"]
        count["r"] += 1
        copy = pltpu.make_async_remote_copy(
            src, dst, send.at[k], recv.at[k], device_id=device(to), device_id_type=MESH
        )
        if start:
            copy.start()
        pending.append(copy)
        return copy

    def near(src, dst):
        k = count["l"]
        count["l"] += 1
        copy = pltpu.make_async_copy(src, dst, local.at[k])
        copy.start()
        return copy

    def columns(q, half, c0, w):
        return pl.ds(pl.multiple_of(q * 1792 + half * 896 + c0, 128), w)

    def chunk_copies(k, q, kind):
        c0, wc, _ = CHUNKS[k]
        i = k * 8 + q
        cols = columns(q, (h, 1 - h)[kind], c0, wc)
        sources = (grad.at[0, :, cols], drift.at[0, :, cols])
        if kind == 0:
            targets = (g_buf[k].at[q, pl.ds(0, 384)], dr_own[k].at[q])
            return [
                pltpu.make_async_copy(sources[j], targets[j], load.at[j, i]) for j in range(2)
            ]
        targets = (g_buf[k].at[q, pl.ds(384, 384)], dr_sib[k].at[q])
        return [
            pltpu.make_async_remote_copy(
                sources[j],
                targets[j],
                load.at[2 + j, i],
                load.at[4 + j, i],
                device_id=device(sib),
                device_id_type=MESH,
            )
            for j in range(2)
        ]

    def start_chunk(k, kind):
        @pl.loop(0, 8)
        def _(q):
            for copy in chunk_copies(k, q, kind):
                copy.start()

    col_own = pl.ds(pl.multiple_of(h * 896, 128), 896)
    col_sib = pl.ds(pl.multiple_of((1 - h) * 896, 128), 896)

    load_act = near(act.at[0], a_own)
    start_chunk(PRODUCTS[0], 0)
    load_x = near(x_in.at[0], x_buf)

    barrier = pltpu.get_barrier_semaphore()
    others = [sib] + [step(at, axis, by) for axis in "xyz" for by in (1, 2, 3)]
    for to in others:
        pl.semaphore_signal(barrier, 1, device_id=device(to), device_id_type=MESH)
    pl.semaphore_wait(barrier, len(others))

    send_act = remote(act.at[0], a_sib, sib)
    start_chunk(PRODUCTS[0], 1)

    load_act.wait()
    for i in range(5):
        at_buf[pl.ds(i * 128, 128), pl.ds(0, 384)] = a_own[:, pl.ds(i * 128, 128)].T
    send_act.wait_recv()
    for i in range(5):
        at_buf[pl.ds(i * 128, 128), pl.ds(384, 384)] = a_sib[:, pl.ds(i * 128, 128)].T

    scale = inner_rate / (384 * 16)

    def product_part(k, first, last):
        c0, wc, parts = CHUNKS[k]

        @pl.loop(first, last)
        def _(q):
            for copy in chunk_copies(k, q, 0):
                copy.wait()
            for copy in chunk_copies(k, q, 1):
                copy.wait_recv()
            dr32[pl.ds(rows_own, 40), pl.ds(0, wc)] = dr_own[k][q].astype(F32)
            dr32[pl.ds(rows_sib, 40), pl.ds(0, wc)] = dr_sib[k][q].astype(F32)
            total = jnp.dot(at_buf[...], g_buf[k][q], preferred_element_type=F32)
            value = (total * scale).astype(BF)
            for part in parts:
                order, pc, w, r0, rows = part
                ref = p_buf[PARTS.index(part)]
                block = value[:, pc - c0 : pc - c0 + w].reshape(4, 2, 80, w)
                ref[q // 2, q % 2] = block[:, :, r0 : r0 + rows]
                mine = (q // 2, q % 2, at["z"], at["y"] % 2)
                ref[mine] = (
                    ref[mine].astype(F32) + dr32[pl.ds(r0, rows), pl.ds(pc - c0, w)]
                ).astype(BF)

    def product(k):
        product_part(k, 0, 4)
        later = PRODUCTS.index(k) + 1
        if later < len(PRODUCTS):
            start_chunk(PRODUCTS[later], 0)
            start_chunk(PRODUCTS[later], 1)
        product_part(k, 4, 8)
        if k == PRODUCTS[0]:
            for copy in state_copies():
                state.append(copy)

    state = []

    def state_copies():
        return (
            near(w_in.at[:, col_own], ow.at[pl.ds(rows_own, 40)]),
            near(m_in.at[:, col_own], om.at[pl.ds(rows_own, 40)]),
            remote(w_in.at[:, col_sib], ow.at[pl.ds(rows_own, 40)], sib),
            remote(m_in.at[:, col_sib], om.at[pl.ds(rows_own, 40)], sib),
        )

    def have_state():
        for i in range(len(state)):
            if i < 2:
                state[i].wait()
            else:
                state[i].wait_recv()
        state.clear()

    def tiles(axes, half_axis, half, body):
        n = 4 ** len(axes) // (1 if half_axis is None else 2)

        @pl.loop(0, n)
        def _(i):
            sel = {}
            for axis in axes:
                if axis == half_axis:
                    sel[axis] = 2 * half + i % 2
                    i = i // 2
                else:
                    sel[axis] = i % 4
                    i = i // 4
            body(sel)

    def pipeline(s):
        order, pc, w, r0, rows = PARTS[s]
        p, wo, st = p_buf[s], w_out[s], stage[s]
        fixed = {}
        for phase in range(2):
            axis = order[phase]
            left_axes = ordered(order[phase + 1 :])
            split = order[-1]
            via, from_left, from_right = ring[s][phase]
            m = at[axis]
            right, left = step(at, axis, 1), step(at, axis, 3)

            def block(dest, half):
                return p.at[index("xyz", {**fixed, axis: dest % 4, split: ("half", half)})]

            def part_of(ref, half):
                return ref.at[index(left_axes, {split: ("half", half)})]

            v0 = remote(block(m + 2, 0), part_of(via, 0), right)
            v1 = remote(block(m + 2, 1), part_of(via, 1), left)
            if phase == 0:
                yield
            e0 = remote(block(m + 1, 1), part_of(from_left, 1), right)
            e1 = remote(block(m + 3, 0), part_of(from_right, 0), left)
            yield
            v0.wait_recv()
            v1.wait_recv()
            for half, dest in ((0, m + 1), (1, m + 3)):

                def add(sel):
                    i = index("xyz", {**fixed, **sel, axis: dest % 4})
                    p[i] = (p[i].astype(F32) + via[index(left_axes, sel)].astype(F32)).astype(BF)

                tiles(left_axes, split, half, add)
            l0 = remote(block(m + 1, 0), part_of(from_left, 0), right)
            l1 = remote(block(m + 3, 1), part_of(from_right, 1), left)
            yield
            for copy in (e0, e1, l0, l1):
                copy.wait_recv()

            def total(sel):
                i = index("xyz", {**fixed, **sel, axis: m})
                j = index(left_axes, sel)
                p[i] = (
                    p[i].astype(F32) + (from_left[j].astype(F32) + from_right[j].astype(F32))
                ).astype(BF)

            tiles(left_axes, None, 0, total)
            fixed[axis] = m
        axis = order[2]
        bufs = ring[s][2]
        got = [
            remote(
                p.at[index("xyz", {**fixed, axis: (at[axis] + by) % 4})],
                bufs[by - 1],
                step(at, axis, by),
            )
            for by in (1, 2, 3)
        ]
        yield
        for copy in got:
            copy.wait_recv()
        have_state()
        me = {"x": at["x"], "y": at["y"], "z": at["z"]}
        mine = index("xyz", me)
        summed = p[mine].astype(F32)
        for ref in bufs:
            summed = summed + ref[...].astype(F32)
        pseudo = summed * 0.125
        area = (pl.ds(r0, rows), pl.ds(pc, w))
        momentum = decay_rate * om[area] + pseudo
        weights = ow[area] - outer_rate * (pseudo + decay_rate * momentum)
        nm[area] = momentum
        nw[area] = weights
        st[...] = weights.astype(BF)

        def tile(sel):
            return wo.at[(h,) + index("xyz", sel)]

        keep = near(st, tile(me))
        got = [remote(st, tile(me), step(at, axis, by)) for by in (1, 2, 3)]
        yield
        keep.wait()
        for copy in got:
            copy.wait_recv()
        split = order[2]
        across = []

        def part(axis, pos, half=None):
            sel = {**fixed, axis: pos % 4}
            if half is not None:
                sel[split] = ("half", half)
            return tile(sel)

        axis = order[1]
        del fixed[axis]
        m = at[axis]
        right, left = step(at, axis, 1), step(at, axis, 3)
        r = remote(part(axis, m), part(axis, m), right)
        l = remote(part(axis, m), part(axis, m), left)
        yield
        r.wait_recv()
        fr = remote(part(axis, m + 3, 0), part(axis, m + 3, 0), right)
        l.wait_recv()
        fl = remote(part(axis, m + 1, 1), part(axis, m + 1, 1), left)
        yield
        fr.wait_recv()
        fl.wait_recv()
        axis = order[0]
        del fixed[axis]
        m = at[axis]
        right, left = step(at, axis, 1), step(at, axis, 3)
        r0_, l1_ = (
            remote(part(axis, m, half), part(axis, m, half), to)
            for half, to in ((0, right), (1, left))
        )
        across.append(remote(part(axis, m), part(axis, m), sib))
        yield
        r1_, l0_ = (
            remote(part(axis, m, half), part(axis, m, half), to)
            for half, to in ((1, right), (0, left))
        )
        yield
        r0_.wait_recv()
        fr = remote(part(axis, m + 3, 0), part(axis, m + 3, 0), right)
        l1_.wait_recv()
        fl = remote(part(axis, m + 1, 1), part(axis, m + 1, 1), left)
        yield
        r1_.wait_recv()
        l0_.wait_recv()
        across.append(remote(part(axis, m + 3), part(axis, m + 3), sib))
        across.append(remote(part(axis, m + 1), part(axis, m + 1), sib))
        yield
        fr.wait_recv()
        fl.wait_recv()
        across.append(remote(part(axis, m + 2), part(axis, m + 2), sib))
        yield
        for copy in across:
            copy.wait_recv()

    runs = []
    first = 0
    for _, _, parts in CHUNKS:
        runs.append([pipeline(first + i) for i in range(len(parts))])
        first += len(parts)

    def go(k, n=1):
        for _ in range(n):
            for run in runs[k]:
                next(run, None)

    def weight_copies(k, q):
        base = sum(len(parts) for _, _, parts in CHUNKS[:k])
        return [
            pltpu.make_async_copy(
                w_out[base + i].at[:, q // 2, q % 2],
                w_load[i].at[:, q // 2, q % 2],
                w_sem.at[k, i * 8 + q],
            )
            for i in range(len(CHUNKS[k][2]))
        ]

    def load_weights(k):
        @pl.loop(0, 8)
        def _(q):
            for copy in weight_copies(k, q):
                copy.start()

    def outputs(k, first, last):
        c0, wc, parts = CHUNKS[k]
        if k == 0 and first == 0:
            load_x.wait()
        refs_of = (w_load, w_mid)[k]
        @pl.loop(first, last)
        def _(q):
            if k == 0:
                for copy in weight_copies(k, q):
                    copy.wait()
            value = jnp.dot(
                x_buf[...], weights_of(parts, refs_of, q), preferred_element_type=F32
            ).astype(BF)
            base, _ = PLACES[k]
            for half in range(2):
                cols = pl.ds(pl.multiple_of((q * 2 + half) * 512 + base, 128), wc)
                o_out[:, cols] = value[:, half * wc : (half + 1) * wc]

    back = []

    def send_back():
        back.append(remote(nw.at[pl.ds(rows_sib, 40)], nw_out.at[:, col_own], sib))
        back.append(remote(nm.at[pl.ds(rows_sib, 40)], nm_out.at[:, col_own], sib))
        nw_out[:, col_own] = nw[pl.ds(rows_own, 40)]
        nm_out[:, col_own] = nm[pl.ds(rows_own, 40)]

    for word in ORDER:
        kind, k = word[0], int(word[1])
        if kind == "p":
            product(k)
        elif kind == "s":
            go(k)
        elif kind == "l":
            load_weights(k)
        elif kind == "m":
            outputs(k, int(word[2]), int(word[3]))
        else:
            send_back()

    for run in sum(runs, []):
        for _ in run:
            pass
    for copy in back:
        copy.wait_recv()
    for copy in pending:
        copy.wait_send()
    for k in range(len(CHUNKS)):

        @pl.loop(0, 8)
        def _(q):
            for copy in chunk_copies(k, q, 1):
                copy.wait_send()


def last_kernel(nw, nm, x, early, w0, w1, w2, nw_out, nm_out, o_out, buf, sem):
    c0, wc, parts = CHUNKS[2]

    def early_copies(q):
        copies = []
        for half in range(2):
            for k, (base, w) in PLACES.items():
                src = pl.ds(pl.multiple_of((q * 2 + half) * 512 + base, 128), w)
                dst = pl.ds(pl.multiple_of(q * 1792 + half * 896 + CHUNKS[k][0], 128), w)
                copies.append(
                    pltpu.make_async_copy(
                        early.at[:, src], o_out.at[0, :, dst], sem.at[2 + q * 6 + half * 2 + k]
                    )
                )
        return copies

    def last_copies(q):
        return [
            pltpu.make_async_copy(
                buf.at[q, :, pl.ds(half * wc, wc)],
                o_out.at[0, :, pl.ds(pl.multiple_of(q * 1792 + half * 896 + c0, 128), wc)],
                sem.at[2 + q * 6 + 4 + half],
            )
            for half in range(2)
        ]

    state = [
        pltpu.make_async_copy(nw, nw_out, sem.at[0]),
        pltpu.make_async_copy(nm, nm_out, sem.at[1]),
    ]
    for copy in state:
        copy.start()

    @pl.loop(0, 8)
    def _(q):
        for copy in early_copies(q):
            copy.start()

    @pl.loop(0, 8)
    def _(q):
        weights = weights_of(parts, (w0, w1, w2), q)
        buf[q] = jnp.dot(x[...], weights, preferred_element_type=F32).astype(BF)
        for copy in last_copies(q):
            copy.start()

    for copy in state:
        copy.wait()

    @pl.loop(0, 8)
    def _(q):
        for copy in early_copies(q) + last_copies(q):
            copy.wait()


def local(activations, output_grad, inner_drift, outer_weights, outer_momentum, next_inputs):
    any_ = pl.BlockSpec(memory_space=pl.ANY)
    vmem = pl.BlockSpec(memory_space=pltpu.VMEM)
    w_shapes = [(2,) + dims("xyz", (rows, w)) for _, _, w, _, rows in PARTS]
    scratch = [
        pltpu.VMEM((384, 640), BF),
        pltpu.VMEM((384, 640), BF),
        pltpu.VMEM((640, 768), BF),
        pltpu.VMEM((80, max(wc for _, wc, _ in CHUNKS)), F32),
    ]
    scratch += [pltpu.VMEM((80, 896), F32)] * 4
    scratch += [pltpu.VMEM(shape, BF) for shape in w_shapes[3:6] + w_shapes[:3]]
    scratch += [pltpu.VMEM((8, 40, wc), BF) for _, wc, _ in CHUNKS] * 2
    scratch += [pltpu.VMEM((8, 768, wc), BF) for _, wc, _ in CHUNKS]
    scratch += [pltpu.VMEM(dims("xyz", (rows, w)), BF) for _, _, w, _, rows in PARTS]
    scratch += [pltpu.VMEM((rows, w), BF) for _, _, w, _, rows in PARTS]
    for order, _, w, _, rows in PARTS:
        for phase in range(3):
            scratch += [pltpu.VMEM(dims(ordered(order[phase + 1 :]), (rows, w)), BF)] * 3
    n_remote = 1 + 2 + 2 + len(PARTS) * 32
    n_local = 2 + 2 + len(PARTS)
    scratch += [
        pltpu.SemaphoreType.DMA((n_remote,)),
        pltpu.SemaphoreType.DMA((n_remote,)),
        pltpu.SemaphoreType.DMA((n_local,)),
        pltpu.SemaphoreType.DMA((6, 8 * len(CHUNKS))),
        pltpu.SemaphoreType.DMA((len(CHUNKS), 8 * 3)),
    ]
    results = pl.pallas_call(
        sync_kernel,
        out_shape=[pltpu.VMEM((40, 1792), F32)] * 2
        + [pltpu.VMEM((384, 640), BF), pltpu.VMEM((384, 16 * 512), BF)]
        + [jax.ShapeDtypeStruct(shape, BF) for shape in w_shapes[:3]]
        + [pltpu.VMEM(shape, BF) for shape in w_shapes[6:]],
        in_specs=[any_] * 6,
        out_specs=[vmem] * 4 + [any_] * 3 + [vmem] * 3,
        scratch_shapes=scratch,
        compiler_params=pltpu.CompilerParams(
            collective_id=0, has_side_effects=True, vmem_limit_bytes=47 * 2**20
        ),
        name="sync",
    )(activations, output_grad, inner_drift, outer_weights, outer_momentum, next_inputs)
    new_weights, new_momentum, inputs_next, early = results[:4]
    state = jax.ShapeDtypeStruct((40, 1792), F32)
    return pl.pallas_call(
        last_kernel,
        out_shape=[state, state, jax.ShapeDtypeStruct((1, 384, 14336), BF)],
        in_specs=[vmem] * 7,
        out_specs=[any_] * 3,
        scratch_shapes=[pltpu.VMEM((8, 384, 768), BF), pltpu.SemaphoreType.DMA((2 + 6 * 8,))],
        compiler_params=pltpu.CompilerParams(vmem_limit_bytes=24 * 2**20),
        name="outputs",
    )(new_weights, new_momentum, inputs_next, early, *results[7:])


def solution(mesh):
    in_specs = (
        P(("rx", "ry"), "node", None),
        P(("rx", "ry"), "node", None),
        P(("rx", "ry"), "node", None),
        P("node", ("rx", "ry")),
        P("node", ("rx", "ry")),
        P(("rx", "ry"), "node", None),
    )
    out_specs = (P("node", ("rx", "ry")), P("node", ("rx", "ry")), P(("rx", "ry"), "node", None))
    return jax.shard_map(local, mesh=mesh, in_specs=in_specs, out_specs=out_specs, check_vma=False)
```

time: 148 us -> 111 us (0.75)
  Pallas kernels: 131 us -> 110 us
  local copies, waits for them, and re-layouts: 15.4 us -> 0 us
    pallas_call x2, Pallas kernels: 131 us -> 110 us  [the longest x1 104 us: local(): pl.pallas_call(sync_kernel, out_shape=[pltpu.VMEM((40, 1792), F32)] * 2 +...]
    unnamed x26 -> x0, local copies, waits for them, and re-layouts: 15.4 us -> none
where the time goes in v2:
time: 111 us
  Pallas kernels  110 us (99%)
    pallas_call x1, Pallas kernels, local(): pl.pallas_call(sync_kernel, out_shape=[pltpu.VMEM((40, 1792), F32)] * 2 +...  104 us
    pallas_call x1, Pallas kernels, local(): pl.pallas_call(last_kernel, out_shape=[state, state, jax.ShapeDtypeStruct...  6.53 us

profile of v2, /device:TPU:1, one launch (start us, length us, event | category | flops | bytes accessed | tf_op | source)
XLA Modules:
  0.0 110.8 jit_solution(3638625639063865095)
XLA Ops:
  0.6 103.7 %sync.1 = (f32[40,1792]{1,0:T(8,128)S(1)}, f32[40,1792]{1,0:T(8,128)S(1)}, bf16[384,640]{1,0:T(8,128)(2,1)S(1)}, bf16[384,8192]{1,0:T(8,128)(2,1)S(1)}, bf16[2,4...) custom-call(bf16[1,384,640]{2,1,0:T(8,128)(2,1)} %refs_0_.1, ...), custom_call_target="tpu_custom_call" | custom-call | tf_op jit(solution)/shard_map/sync/pallas_call | solution.py:571
  104.3 6.5 %outputs.1 = (f32[40,1792]{1,0:T(8,128)}, f32[40,1792]{1,0:T(8,128)}, bf16[1,384,14336]{2,1,0:T(8,128)(2,1)}) custom-call(f32[40,1792]{1,0:T(8,128)S(1)} %get-tuple-element.10.nw, f32[40,1792]{1,0:T(8,128)S(1)} %get-tuple-element.11.nm, bf16[384,640]{1,0:T(8,128)(2,1)S(1)} %get-tuple-element.12.x, bf16[384,8192]{1,0:T(8,128)(2,1)S(1)} %get-tuple-element.13.early, ...), custom_call_target="tpu_custom_call" | custom-call | tf_op jit(solution)/shard_map/outputs/pallas_call | solution.py:587

commit v3 on v2

--- a/solution.py
+++ b/solution.py
@@ -23,10 +23,10 @@
 PARTS = tuple(part for _, _, parts in CHUNKS for part in parts)
 PLACES = {0: (0, 384), 1: (384, 128)}
 ORDER = (
-    "p0", "s0", "p1", "s1", "s0", "s0", "s1", "s1", "p2", "s0", "s1", "s0", "s2", "s1", "s0",
-    "s2", "s0", "s1", "s2", "s1", "s0", "s2", "s0", "s1", "s2", "s0", "s1", "s2", "s0", "s2",
-    "b0", "s0", "s0", "s2", "s1", "s0", "s2", "s1", "s1", "s2", "s2", "s1", "s0", "s1", "l0",
-    "s2", "m004", "s1", "m102", "s2", "m046", "m126", "s2", "m168", "m068", "s2",
+    "p0", "s0", "s0", "p1", "s0", "s1", "s1", "p2", "s0", "s1", "s0", "s2", "s0", "s2", "s0",
+    "s2", "s0", "s1", "s2", "s1", "s0", "s2", "s1", "s0", "s1", "s2", "s0", "s1", "s2", "b0",
+    "s0", "s1", "s2", "s0", "s0", "s1", "s2", "s1", "s0", "s1", "s2", "s1", "s2", "s1", "m002",
+    "s1", "m024", "m102", "s2", "s2", "m048", "s2", "m128", "s2",
 )
 PRODUCTS = tuple(int(word[1]) for word in ORDER if word[0] == "p")
 
@@ -99,20 +99,19 @@
     act, grad, drift, w_in, m_in, x_in = refs[:6]
     nw_out, nm_out, x_buf, o_out = refs[6:10]
     rest = list(refs[10:])
-    w_far = [rest.pop(0) for _ in CHUNKS[0][2]]
     w_last = [rest.pop(0) for _ in CHUNKS[2][2]]
     a_own, a_sib, at_buf, dr32, ow, om, nw, nm = rest[:8]
     del rest[:8]
     w_mid = [rest.pop(0) for _ in CHUNKS[1][2]]
-    w_out = w_far + w_mid + w_last
-    w_load = [rest.pop(0) for _ in CHUNKS[0][2]]
+    w_first = [rest.pop(0) for _ in CHUNKS[0][2]]
+    w_out = w_first + w_mid + w_last
     dr_own = [rest.pop(0) for _ in CHUNKS]
     dr_sib = [rest.pop(0) for _ in CHUNKS]
     g_buf = [rest.pop(0) for _ in CHUNKS]
     p_buf = [rest.pop(0) for _ in PARTS]
     stage = [rest.pop(0) for _ in PARTS]
     ring = [[[rest.pop(0) for _ in range(3)] for _ in range(3)] for _ in PARTS]
-    send, recv, local, load, w_sem = rest
+    send, recv, local, load = rest
 
     at = place()
     h = at["c"]
@@ -177,7 +176,7 @@
 
     load_act = near(act.at[0], a_own)
     start_chunk(PRODUCTS[0], 0)
-    load_x = near(x_in.at[0], x_buf)
+    waiting = [near(x_in.at[0], x_buf)]
 
     barrier = pltpu.get_barrier_semaphore()
     others = [sib] + [step(at, axis, by) for axis in "xyz" for by in (1, 2, 3)]
@@ -200,25 +199,31 @@
     def product_part(k, first, last):
         c0, wc, parts = CHUNKS[k]
 
-        @pl.loop(first, last)
-        def _(q):
-            for copy in chunk_copies(k, q, 0):
-                copy.wait()
-            for copy in chunk_copies(k, q, 1):
-                copy.wait_recv()
-            dr32[pl.ds(rows_own, 40), pl.ds(0, wc)] = dr_own[k][q].astype(F32)
-            dr32[pl.ds(rows_sib, 40), pl.ds(0, wc)] = dr_sib[k][q].astype(F32)
-            total = jnp.dot(at_buf[...], g_buf[k][q], preferred_element_type=F32)
+        @pl.loop(first // 2, last // 2)
+        def _(x):
+            for y in range(2):
+                q = 2 * x + y
+                for copy in chunk_copies(k, q, 0):
+                    copy.wait()
+                for copy in chunk_copies(k, q, 1):
+                    copy.wait_recv()
+            both = jnp.concatenate([g_buf[k][2 * x], g_buf[k][2 * x + 1]], axis=1)
+            total = jnp.dot(at_buf[...], both, preferred_element_type=F32)
             value = (total * scale).astype(BF)
-            for part in parts:
-                order, pc, w, r0, rows = part
-                ref = p_buf[PARTS.index(part)]
-                block = value[:, pc - c0 : pc - c0 + w].reshape(4, 2, 80, w)
-                ref[q // 2, q % 2] = block[:, :, r0 : r0 + rows]
-                mine = (q // 2, q % 2, at["z"], at["y"] % 2)
-                ref[mine] = (
-                    ref[mine].astype(F32) + dr32[pl.ds(r0, rows), pl.ds(pc - c0, w)]
-                ).astype(BF)
+            for y in range(2):
+                q = 2 * x + y
+                dr32[pl.ds(rows_own, 40), pl.ds(0, wc)] = dr_own[k][q].astype(F32)
+                dr32[pl.ds(rows_sib, 40), pl.ds(0, wc)] = dr_sib[k][q].astype(F32)
+                for part in parts:
+                    order, pc, w, r0, rows = part
+                    ref = p_buf[PARTS.index(part)]
+                    start = y * wc + pc - c0
+                    block = value[:, start : start + w].reshape(4, 2, 80, w)
+                    ref[x, y] = block[:, :, r0 : r0 + rows]
+                    mine = (x, y, at["z"], at["y"] % 2)
+                    ref[mine] = (
+                        ref[mine].astype(F32) + dr32[pl.ds(r0, rows), pl.ds(pc - c0, w)]
+                    ).astype(BF)
 
     def product(k):
         product_part(k, 0, 4)
@@ -252,7 +257,7 @@
     def tiles(axes, half_axis, half, body):
         n = 4 ** len(axes) // (1 if half_axis is None else 2)
 
-        @pl.loop(0, n)
+        @pl.loop(0, n, unroll=min(n, 4))
         def _(i):
             sel = {}
             for axis in axes:
@@ -295,7 +300,7 @@
 
                 def add(sel):
                     i = index("xyz", {**fixed, **sel, axis: dest % 4})
-                    p[i] = (p[i].astype(F32) + via[index(left_axes, sel)].astype(F32)).astype(BF)
+                    p[i] = p[i] + via[index(left_axes, sel)]
 
                 tiles(left_axes, split, half, add)
             l0 = remote(block(m + 1, 0), part_of(from_left, 0), right)
@@ -415,33 +420,13 @@
             for run in runs[k]:
                 next(run, None)
 
-    def weight_copies(k, q):
-        base = sum(len(parts) for _, _, parts in CHUNKS[:k])
-        return [
-            pltpu.make_async_copy(
-                w_out[base + i].at[:, q // 2, q % 2],
-                w_load[i].at[:, q // 2, q % 2],
-                w_sem.at[k, i * 8 + q],
-            )
-            for i in range(len(CHUNKS[k][2]))
-        ]
-
-    def load_weights(k):
-        @pl.loop(0, 8)
-        def _(q):
-            for copy in weight_copies(k, q):
-                copy.start()
-
     def outputs(k, first, last):
         c0, wc, parts = CHUNKS[k]
-        if k == 0 and first == 0:
-            load_x.wait()
-        refs_of = (w_load, w_mid)[k]
+        while waiting:
+            waiting.pop().wait()
+        refs_of = (w_first, w_mid)[k]
         @pl.loop(first, last)
         def _(q):
-            if k == 0:
-                for copy in weight_copies(k, q):
-                    copy.wait()
             value = jnp.dot(
                 x_buf[...], weights_of(parts, refs_of, q), preferred_element_type=F32
             ).astype(BF)
@@ -464,8 +449,6 @@
             product(k)
         elif kind == "s":
             go(k)
-        elif kind == "l":
-            load_weights(k)
         elif kind == "m":
             outputs(k, int(word[2]), int(word[3]))
         else:
@@ -524,7 +507,7 @@
         for copy in early_copies(q):
             copy.start()
 
-    @pl.loop(0, 8)
+    @pl.loop(0, 8, unroll=4)
     def _(q):
         weights = weights_of(parts, (w0, w1, w2), q)
         buf[q] = jnp.dot(x[...], weights, preferred_element_type=F32).astype(BF)
@@ -566,16 +549,14 @@
         pltpu.SemaphoreType.DMA((n_remote,)),
         pltpu.SemaphoreType.DMA((n_local,)),
         pltpu.SemaphoreType.DMA((6, 8 * len(CHUNKS))),
-        pltpu.SemaphoreType.DMA((len(CHUNKS), 8 * 3)),
     ]
     results = pl.pallas_call(
         sync_kernel,
         out_shape=[pltpu.VMEM((40, 1792), F32)] * 2
         + [pltpu.VMEM((384, 640), BF), pltpu.VMEM((384, 16 * 512), BF)]
-        + [jax.ShapeDtypeStruct(shape, BF) for shape in w_shapes[:3]]
         + [pltpu.VMEM(shape, BF) for shape in w_shapes[6:]],
         in_specs=[any_] * 6,
-        out_specs=[vmem] * 4 + [any_] * 3 + [vmem] * 3,
+        out_specs=[vmem] * 7,
         scratch_shapes=scratch,
         compiler_params=pltpu.CompilerParams(
             collective_id=0, has_side_effects=True, vmem_limit_bytes=47 * 2**20
@@ -592,7 +573,7 @@
         scratch_shapes=[pltpu.VMEM((8, 384, 768), BF), pltpu.SemaphoreType.DMA((2 + 6 * 8,))],
         compiler_params=pltpu.CompilerParams(vmem_limit_bytes=24 * 2**20),
         name="outputs",
-    )(new_weights, new_momentum, inputs_next, early, *results[7:])
+    )(new_weights, new_momentum, inputs_next, early, *results[4:])
 
 
 def solution(mesh):

time: 111 us -> 106 us (0.955)
  Pallas kernels: 110 us -> 105 us
    pallas_call x1, Pallas kernels: 104 us -> 99.2 us  [local(): pl.pallas_call(sync_kernel, out_shape=[pltpu.VMEM((40, 1792), F32)] * 2 +...]
where the time goes in v3:
time: 106 us; the launch traced here: 105 us
  Pallas kernels  105 us (99%)
    pallas_call x1, Pallas kernels, local(): pl.pallas_call(sync_kernel, out_shape=[pltpu.VMEM((40, 1792), F32)] * 2 +...  99.2 us
    pallas_call x1, Pallas kernels, local(): pl.pallas_call(last_kernel, out_shape=[state, state, jax.ShapeDtypeStruct...  5.47 us

profile of v3, /device:TPU:1, one launch (start us, length us, event | category | flops | bytes accessed | tf_op | source)
XLA Modules:
  0.0 105.5 jit_solution(7797315265118043014)
XLA Ops:
  0.6 99.2 %sync.1 = (f32[40,1792]{1,0:T(8,128)S(1)}, f32[40,1792]{1,0:T(8,128)S(1)}, bf16[384,640]{1,0:T(8,128)(2,1)S(1)}, bf16[384,8192]{1,0:T(8,128)(2,1)S(1)}, bf16[2,4...) custom-call(bf16[1,384,640]{2,1,0:T(8,128)(2,1)} %refs_0_.1, ...), custom_call_target="tpu_custom_call" | custom-call | tf_op jit(solution)/shard_map/sync/pallas_call | solution.py:553
  99.8 5.5 %outputs.1 = (f32[40,1792]{1,0:T(8,128)}, f32[40,1792]{1,0:T(8,128)}, bf16[1,384,14336]{2,1,0:T(8,128)(2,1)}) custom-call(f32[40,1792]{1,0:T(8,128)S(1)} %get-tuple-element.10.nw, f32[40,1792]{1,0:T(8,128)S(1)} %get-tuple-element.11.nm, bf16[384,640]{1,0:T(8,128)(2,1)S(1)} %get-tuple-element.12.x, bf16[384,8192]{1,0:T(8,128)(2,1)S(1)} %get-tuple-element.13.early, ...), custom_call_target="tpu_custom_call" | custom-call | tf_op jit(solution)/shard_map/outputs/pallas_call | solution.py:568
